TPU v7x, 32 devices: a whole 2x2x4 slice. The times are simulated.
32 devices in a mesh: grp: 2 (over x), ep: 16 (over z, y, core).
Axes of the slice: x: 2, y: 2, z: 4, core: 2. Of those that a mesh axis runs over, the one named last changes fastest.
Arguments:
- tokens: bfloat16 [4096, 2048], P(('grp', 'ep')), parts along dimension 0, may hold values from -6 to 6
- cotangent: bfloat16 [4096, 2048], P(('grp', 'ep')), parts along dimension 0, may hold values from -18 to 18
- expert_ids: int32 [4096, 8], P(('grp', 'ep')), parts along dimension 0, may hold values from 0 to 15, all different within a row; in each aligned block of 128 rows (0 to 127, 128 to 255, ...) at most 72 rows name the same one
- routing: bfloat16 [4096, 8], P(('grp', 'ep')), parts along dimension 0, may hold values from 0.019897461 to 0.5
- gate_proj: bfloat16 [16, 2048, 384], P('ep'), may hold values from -0.125 to 0.125
- up_proj: bfloat16 [16, 2048, 384], P('ep'), may hold values from -0.125 to 0.125
- down_proj: bfloat16 [16, 384, 2048], P('ep'), may hold values from -0.3125 to 0.3125
Outputs:
- grad_tokens: bfloat16 [4096, 2048], P(('grp', 'ep')), parts along dimension 0
- grad_routing: bfloat16 [4096, 8], P(('grp', 'ep')), parts along dimension 0
- grad_gate: bfloat16 [32, 2048, 384], P(('grp', 'ep')), parts along dimension 0
- grad_up: bfloat16 [32, 2048, 384], P(('grp', 'ep')), parts along dimension 0
- grad_down: bfloat16 [32, 384, 2048], P(('grp', 'ep')), parts along dimension 0
There are 2 independent parts, one for each index of `grp`. A program takes and returns all parts, laid end to end along the dimension named above; an argument that names none is the same for every part. Nothing has to cross between parts.
Inputs may be any that keep to these rules, and one draw needn't show every extreme that they name: `expert_ids`: each row names 8 different experts; among the 128 rows of one device no expert is named by more than 72 rows, a bound that some block reaches.
All inputs are finite; a program needn't handle non-finite values.
Results may differ from a plain program's by a relative error of at most 0.0058.
Values may be sent and summed in bfloat16 or wider, within the bound.
A program may use at most 128 MiB of HBM per device.

v0:
```python
import jax
import jax.numpy as jnp
from jax import lax
from jax.sharding import PartitionSpec as P


def contract_last(left, right):
    return lax.dot_general(
        left, right, (((1,), (1,)), ((), ())), preferred_element_type=jnp.float32
    )


def contract_first(left, right):
    return lax.dot_general(
        left, right, (((0,), (0,)), ((), ())), preferred_element_type=jnp.float32
    )


def expert_rows(rows_in, cotangent_rows, weight_in, gate_w, up_w, down_w):
    gate_pre = jnp.dot(rows_in, gate_w, preferred_element_type=jnp.float32)
    up_pre = jnp.dot(rows_in, up_w, preferred_element_type=jnp.float32)
    gate_sigmoid = jax.nn.sigmoid(gate_pre)
    activated = gate_pre * gate_sigmoid
    hidden = activated * up_pre
    hidden_raw = contract_last(cotangent_rows, down_w)
    delta_prob = jnp.sum(hidden * hidden_raw, axis=-1).astype(jnp.bfloat16)
    scale_col = weight_in.astype(jnp.float32)[:, None]
    hidden_grad = scale_col * hidden_raw
    up_grad = (hidden_grad * activated).astype(jnp.bfloat16)
    gate_grad = (
        hidden_grad * up_pre * gate_sigmoid * (1.0 + gate_pre * (1.0 - gate_sigmoid))
    ).astype(jnp.bfloat16)
    grad_rows = (contract_last(gate_grad, gate_w) + contract_last(up_grad, up_w)).astype(
        jnp.bfloat16
    )
    scaled_hidden = (scale_col * hidden).astype(jnp.bfloat16)
    return (grad_rows, delta_prob, gate_grad, up_grad, scaled_hidden)


def local(tokens, cotangent, expert_ids, routing, gate_proj, up_proj, down_proj):
    peers = lax.axis_size("ep")
    tok_rows, model_width = tokens.shape
    choose = expert_ids.shape[1]
    assigned = tok_rows * choose
    capacity = assigned // peers + max(1, assigned // (8 * peers))
    total_rows = peers * capacity
    flat_ids = expert_ids.reshape(-1)
    matches = (flat_ids[:, None] == jnp.arange(peers, dtype=jnp.int32)[None, :]).astype(jnp.int32)
    slot_index = jnp.sum(
        (jnp.cumsum(matches, axis=0, dtype=jnp.int32) - matches) * matches, axis=1, dtype=jnp.int32
    )
    target = flat_ids * capacity + slot_index
    owner_row = jnp.arange(assigned, dtype=jnp.int32) // choose
    send_rows = jnp.zeros((total_rows, model_width), jnp.bfloat16).at[target].set(tokens[owner_row])
    send_cotangent = (
        jnp.zeros((total_rows, model_width), jnp.bfloat16).at[target].set(cotangent[owner_row])
    )
    send_weight = jnp.zeros((total_rows,), jnp.bfloat16).at[target].set(routing.reshape(-1))
    send_rows = send_rows.reshape(peers, capacity, model_width)
    send_cotangent = send_cotangent.reshape(peers, capacity, model_width)
    send_weight = send_weight.reshape(peers, capacity)
    gate_w = gate_proj[0]
    up_w = up_proj[0]
    down_w = down_proj[0]
    hidden_width = gate_w.shape[1]
    rows_in = lax.all_to_all(send_rows, "ep", split_axis=0, concat_axis=0, tiled=True)
    cotangent_in = lax.all_to_all(send_cotangent, "ep", split_axis=0, concat_axis=0, tiled=True)
    weight_in = lax.all_to_all(send_weight, "ep", split_axis=0, concat_axis=0, tiled=True)
    count = rows_in.shape[1]
    grad_rows, delta_prob, gate_grad, up_grad, scaled_hidden = expert_rows(
        rows_in.reshape(-1, model_width),
        cotangent_in.reshape(-1, model_width),
        weight_in.reshape(-1),
        gate_w,
        up_w,
        down_w,
    )
    back_rows = lax.all_to_all(
        grad_rows.reshape(peers, count, model_width), "ep", split_axis=0, concat_axis=0, tiled=True
    )
    back_prob = lax.all_to_all(
        delta_prob.reshape(peers, count), "ep", split_axis=0, concat_axis=0, tiled=True
    )
    recv_rows, recv_cotangent, gate_grad, up_grad, scaled_hidden, back_rows, back_prob = (
        rows_in,
        cotangent_in,
        gate_grad.reshape(peers, count, hidden_width),
        up_grad.reshape(peers, count, hidden_width),
        scaled_hidden.reshape(peers, count, hidden_width),
        back_rows,
        back_prob,
    )
    inputs_all = recv_rows.reshape(total_rows, model_width)
    cotangent_all = recv_cotangent.reshape(total_rows, model_width)
    gate_grad = gate_grad.reshape(total_rows, hidden_width)
    up_grad = up_grad.reshape(total_rows, hidden_width)
    scaled_hidden = scaled_hidden.reshape(total_rows, hidden_width)
    grad_gate = contract_first(inputs_all, gate_grad).astype(jnp.bfloat16)[None]
    grad_up = contract_first(inputs_all, up_grad).astype(jnp.bfloat16)[None]
    grad_down = contract_first(scaled_hidden, cotangent_all).astype(jnp.bfloat16)[None]
    back_flat = back_rows.reshape(total_rows, model_width)
    assignment_grad = back_flat[target].astype(jnp.float32).reshape(tok_rows, choose, model_width)
    grad_tokens = jnp.sum(assignment_grad, axis=1).astype(jnp.bfloat16)
    grad_routing = back_prob.reshape(-1)[target].reshape(tok_rows, choose)
    return (grad_tokens, grad_routing, grad_gate, grad_up, grad_down)


def solution(mesh):
    return jax.shard_map(
        local,
        mesh=mesh,
        in_specs=(
            P(("grp", "ep"), None),
            P(("grp", "ep"), None),
            P(("grp", "ep"), None),
            P(("grp", "ep"), None),
            P("ep", None, None),
            P("ep", None, None),
            P("ep", None, None),
        ),
        out_specs=(
            P(("grp", "ep"), None),
            P(("grp", "ep"), None),
            P(("grp", "ep"), None, None),
            P(("grp", "ep"), None, None),
            P(("grp", "ep"), None, None),
        ),
        check_vma=False,
    )
```

profile of v0, /device:TPU:15, one launch (start us, length us, event | category | flops | bytes accessed | tf_op | source)
XLA Modules:
  0.0 416.6 jit_solution(12771676623892888035)
XLA Ops:
  0.6 0.8 broadcast_multiply_fusion
  3.5 4.5 %reduce-window.6 = s32[16,8,128]{2,1,0:T(8,128)S(1)} reduce-window(s32[16,8,128]{2,1,0:T(8,128)S(1)} %fusion.25, s32[]{:T(128)} %constant.29.clone.1), window={size=1x1x128 pad=0_0x0_0x127_0}, to_apply=%region_0.0 | reduce-window | flops 2080768 | bytes 131076 | tf_op jit(solution)/shard_map/reduce-window
  8.5 7.6 %scatter_custom_fusion = bf16[1152]{0:T(1024)(128)(2,1)S(1)} fusion(s32[1024]{0:T(1024)S(1)} %bitcast.69, bf16[1024]{0:T(1024)(128)(2,1)S(1)} %reshape.206, bf16[]{:T(256)} %constant.27.clone.1), kind=kCustom, calls=%fused_computation.57 | custom fusion | bytes 2306 | tf_op jit(solution)/shard_map/scatter | solution.py:58
  16.8 7.2 %all-to-all-start = ((bf16[16,1,72]{2,1,0:T(2,128)(2,1)}), bf16[16,1,72]{2,1,0:T(2,128)(2,1)S(1)}, u32[]{:S(2)}, u32[]{:S(2)}) async-start(bf16[16,1,72]{2,1,0:T(2,128)(2,1)} %all_to_all.25), calls=%async_computation | async-start | bytes 16384 | tf_op jit(solution)/shard_map/all_to_all | solution.py:68
  24.0 23.6 %scatter_custom_fusion.2 = bf16[1152,2048]{1,0:T(8,128)(2,1)} fusion(s32[1024]{0:T(1024)S(1)} %bitcast.70, bf16[128,2048]{1,0:T(8,128)(2,1)} %param.7, s32[1024]{0:T(1024)S(1)} %broadcast_clamp_fusion.1, bf16[]{:T(256)} %constant.27.clone.1), kind=kCustom, calls=%fused_computation.10 | custom fusion | bytes 4719104 | tf_op jit(solution)/shard_map/scatter | solution.py:54
  47.6 6.3 %all-to-all-start.2 = ((bf16[16,72,2048]{2,1,0:T(8,128)(2,1)}), bf16[16,72,2048]{2,1,0:T(8,128)(2,1)}, u32[]{:S(2)}, u32[]{:S(2)}) async-start(bf16[16,72,2048]{2,1,0:T(8,128)(2,1)} %bitcast.64), calls=%async_computation.2 | async-start | bytes 9437184 | tf_op jit(solution)/shard_map/all_to_all | solution.py:66
  53.9 23.5 %scatter_custom_fusion.1 = bf16[1152,2048]{1,0:T(8,128)(2,1)} fusion(s32[1024]{0:T(1024)S(1)} %bitcast.71, bf16[128,2048]{1,0:T(8,128)(2,1)} %param.8, s32[1024]{0:T(1024)S(1)} %broadcast_clamp_fusion.1, bf16[]{:T(256)} %constant.27.clone.1), kind=kCustom, calls=%fused_computation.12 | custom fusion | bytes 4719104 | tf_op jit(solution)/shard_map/scatter | solution.py:56
  77.5 80.0 %all-to-all-done.2 = bf16[16,72,2048]{2,1,0:T(8,128)(2,1)} async-done(((bf16[16,72,2048]{2,1,0:T(8,128)(2,1)}), bf16[16,72,2048]{2,1,0:T(8,128)(2,1)}, u32[]{:S(2)}, u32[]{:S(2)}) %all-to-all-start.2) | async-done | bytes 4718624 | tf_op jit(solution)/shard_map/all_to_all | solution.py:66
  157.5 5.2 %all-to-all-start.1 = ((bf16[16,72,2048]{2,1,0:T(8,128)(2,1)}), bf16[16,72,2048]{2,1,0:T(8,128)(2,1)}, u32[]{:S(2)}, u32[]{:S(2)}) async-start(bf16[16,72,2048]{2,1,0:T(8,128)(2,1)} %bitcast.63), calls=%async_computation.1 | async-start | bytes 9437184 | tf_op jit(solution)/shard_map/all_to_all | solution.py:67
  162.9 6.0 %fusion.13 = f32[1152,384]{0,1:T(8,128)} fusion(bf16[1152,2048]{1,0:T(8,128)(2,1)} %bitcast.9, bf16[1,2048,384]{2,1,0:T(8,128)(2,1)S(1)} %copy-done), kind=kOutput, calls=%fused_computation.30 | convolution fusion | flops 1811939328 | bytes 8060928 | tf_op jit(solution)/shard_map/dot_general | solution.py:20
  168.9 5.8 %fusion.16 = f32[1152,384]{0,1:T(8,128)} fusion(bf16[1152,2048]{1,0:T(8,128)(2,1)} %bitcast.9, bf16[1,2048,384]{2,1,0:T(8,128)(2,1)S(1)} %copy-done.1), kind=kOutput, calls=%fused_computation.33 | convolution fusion | flops 1811939328 | bytes 8060928 | tf_op jit(solution)/shard_map/dot_general | solution.py:21
  174.7 91.6 %all-to-all-done.1 = bf16[16,72,2048]{2,1,0:T(8,128)(2,1)} async-done(((bf16[16,72,2048]{2,1,0:T(8,128)(2,1)}), bf16[16,72,2048]{2,1,0:T(8,128)(2,1)}, u32[]{:S(2)}, u32[]{:S(2)}) %all-to-all-start.1) | async-done | bytes 4718624 | tf_op jit(solution)/shard_map/all_to_all | solution.py:67
  266.3 7.8 %multiply_reduce_fusion = (bf16[1152]{0:T(1024)(128)(2,1)S(1)}, bf16[1152,384]{0,1:T(8,128)(2,1)}, bf16[1152,384]{0,1:T(8,128)(2,1)}) fusion(f32[1152,384]{0,1:T(8,128)} %fusion.16, f32[1152,384]{0,1:T(8,128)} %fusion.13, f32[1152]{0:T(1024)S(1)} %reshape.169, bf16[1152,2048]{1,0:T(8,128)(2,1)} %bitcast.6, bf16[1,384,2048]{2,1,0:T(8,128)(2,1)} %param.13), kind=kOutput, calls=%fused_computation.23 | convolution fusion | flops 1819458432 | bytes 11606784 | tf_op jit(solution)/shard_map/dot_general | solution.py:8
  274.9 4.9 %all-to-all-start.4 = ((bf16[16,1,72]{2,1,0:T(2,128)(2,1)}), bf16[16,1,72]{2,1,0:T(2,128)(2,1)S(1)}, u32[]{:S(2)}, u32[]{:S(2)}) async-start(bf16[16,1,72]{2,1,0:T(2,128)(2,1)} %convert_element_type.69), calls=%async_computation.4 | async-start | bytes 16384 | tf_op jit(solution)/shard_map/all_to_all | solution.py:81
  279.8 3.9 fusion.11
  283.7 4.4 %fusion = bf16[1152,2048]{1,0:T(8,128)(2,1)} fusion(f32[1152,2048]{1,0:T(8,128)S(1)} %fusion.11, bf16[1152,384]{0,1:T(8,128)(2,1)S(1)} %copy-done.3, bf16[1,2048,384]{2,1,0:T(8,128)(2,1)S(1)} %copy-done.1), kind=kOutput, calls=%fused_computation.8 | convolution fusion | flops 1816657920 | bytes 16613376 | tf_op jit(solution)/shard_map/dot_general | solution.py:8
  288.1 6.5 %all-to-all-start.3 = ((bf16[16,72,2048]{2,1,0:T(8,128)(2,1)}), bf16[16,72,2048]{2,1,0:T(8,128)(2,1)}, u32[]{:S(2)}, u32[]{:S(2)}) async-start(bf16[16,72,2048]{2,1,0:T(8,128)(2,1)} %bitcast.65), calls=%async_computation.3 | async-start | bytes 9437184 | tf_op jit(solution)/shard_map/all_to_all | solution.py:78
  294.7 6.4 %fusion.5 = bf16[1,2048,384]{2,1,0:T(8,128)(2,1)} fusion(bf16[1152,2048]{1,0:T(8,128)(2,1)} %bitcast.9, bf16[1152,384]{0,1:T(8,128)(2,1)S(1)} %copy-done.2), kind=kOutput, calls=%fused_computation.17 | convolution fusion | flops 1812725760 | bytes 7176192 | tf_op jit(solution)/shard_map/dot_general | solution.py:14
  301.0 6.5 %fusion.6 = bf16[1,2048,384]{2,1,0:T(8,128)(2,1)} fusion(bf16[1152,2048]{1,0:T(8,128)(2,1)} %bitcast.9, bf16[1152,384]{0,1:T(8,128)(2,1)S(1)} %copy-done.4), kind=kOutput, calls=%fused_computation.18 | convolution fusion | flops 1812725760 | bytes 7176192 | tf_op jit(solution)/shard_map/dot_general | solution.py:14
  307.5 5.8 %fusion.7 = bf16[1,384,2048]{2,1,0:T(8,128)(2,1)} fusion(bf16[1152,2048]{1,0:T(8,128)(2,1)} %bitcast.6, f32[1152]{0:T(1024)S(1)} %reshape.169, f32[1152,384]{0,1:T(8,128)S(1)} %copy-done.6, f32[1152,384]{0,1:T(8,128)S(1)} %copy-done.5), kind=kOutput, calls=%fused_computation.19 | convolution fusion | flops 1815822336 | bytes 9835008 | tf_op jit(solution)/shard_map/dot_general | solution.py:14
  313.4 6.8 %gather_fusion.1 = bf16[1024]{0:T(1024)(128)(2,1)S(1)} fusion(bf16[1152]{0:T(1024)(128)(2,1)S(1)} %reshape.167, s32[1024]{0:T(1024)S(1)} %broadcast_clamp_fusion), kind=kCustom, calls=%fused_computation.3 | custom fusion | bytes 8192 | tf_op jit(solution)/shard_map/gather | solution.py:104
  321.0 77.2 %all-to-all-done.3 = bf16[16,72,2048]{2,1,0:T(8,128)(2,1)} async-done(((bf16[16,72,2048]{2,1,0:T(8,128)(2,1)}), bf16[16,72,2048]{2,1,0:T(8,128)(2,1)}, u32[]{:S(2)}, u32[]{:S(2)}) %all-to-all-start.3) | async-done | bytes 4718624 | tf_op jit(solution)/shard_map/all_to_all | solution.py:78
  398.2 12.0 %gather_fusion = bf16[1024,2048]{1,0:T(8,128)(2,1)} fusion(bf16[1152,2048]{1,0:T(8,128)(2,1)} %bitcast.13, s32[1024]{0:T(1024)S(1)} %broadcast_clamp_fusion), kind=kCustom, calls=%fused_computation.2 | custom fusion | bytes 8392704 | tf_op jit(solution)/shard_map/gather | solution.py:102
  410.2 5.9 %bitcast_reduce_fusion = bf16[128,2048]{1,0:T(8,128)(2,1)} fusion(bf16[1024,2048]{1,0:T(8,128)(2,1)} %gather_fusion), kind=kLoop, calls=%fused_computation.9 | loop fusion | flops 1835008 | bytes 4718592 | tf_op jit(solution)/shard_map/reduce_sum | solution.py:103
  (43 shorter events, 5.0 us)
Async XLA Ops:
  0.6 162.2 %copy-start = (bf16[1,2048,384]{2,1,0:T(8,128)(2,1)S(1)}, bf16[1,2048,384]{2,1,0:T(8,128)(2,1)}, u32[]{:S(2)}) copy-start(bf16[1,2048,384]{2,1,0:T(8,128)(2,1)} %param.11) | copy-start | bytes 4718596
  16.8 30.8 %all-to-all-start = ((bf16[16,1,72]{2,1,0:T(2,128)(2,1)}), bf16[16,1,72]{2,1,0:T(2,128)(2,1)S(1)}, u32[]{:S(2)}, u32[]{:S(2)}) async-start(bf16[16,1,72]{2,1,0:T(2,128)(2,1)} %all_to_all.25), calls=%async_computation | async-start | bytes 16384 | tf_op jit(solution)/shard_map/all_to_all | solution.py:68
  47.6 109.9 %all-to-all-start.2 = ((bf16[16,72,2048]{2,1,0:T(8,128)(2,1)}), bf16[16,72,2048]{2,1,0:T(8,128)(2,1)}, u32[]{:S(2)}, u32[]{:S(2)}) async-start(bf16[16,72,2048]{2,1,0:T(8,128)(2,1)} %bitcast.64), calls=%async_computation.2 | async-start | bytes 9437184 | tf_op jit(solution)/shard_map/all_to_all | solution.py:66
  157.5 108.8 %all-to-all-start.1 = ((bf16[16,72,2048]{2,1,0:T(8,128)(2,1)}), bf16[16,72,2048]{2,1,0:T(8,128)(2,1)}, u32[]{:S(2)}, u32[]{:S(2)}) async-start(bf16[16,72,2048]{2,1,0:T(8,128)(2,1)} %bitcast.63), calls=%async_computation.1 | async-start | bytes 9437184 | tf_op jit(solution)/shard_map/all_to_all | solution.py:67
  162.9 6.0 %copy-start.1 = (bf16[1,2048,384]{2,1,0:T(8,128)(2,1)S(1)}, bf16[1,2048,384]{2,1,0:T(8,128)(2,1)}, u32[]{:S(2)}) copy-start(bf16[1,2048,384]{2,1,0:T(8,128)(2,1)} %param.12) | copy-start | bytes 4718596
  274.9 13.2 %all-to-all-start.4 = ((bf16[16,1,72]{2,1,0:T(2,128)(2,1)}), bf16[16,1,72]{2,1,0:T(2,128)(2,1)S(1)}, u32[]{:S(2)}, u32[]{:S(2)}) async-start(bf16[16,1,72]{2,1,0:T(2,128)(2,1)} %convert_element_type.69), calls=%async_computation.4 | async-start | bytes 16384 | tf_op jit(solution)/shard_map/all_to_all | solution.py:81
  279.7 3.9 copy-start.3
  288.1 6.6 %copy-start.2 = (bf16[1152,384]{0,1:T(8,128)(2,1)S(1)}, bf16[1152,384]{0,1:T(8,128)(2,1)}, u32[]{:S(2)}) copy-start(bf16[1152,384]{0,1:T(8,128)(2,1)} %get-tuple-element.16) | copy-start | bytes 2654212
  288.1 110.1 %all-to-all-start.3 = ((bf16[16,72,2048]{2,1,0:T(8,128)(2,1)}), bf16[16,72,2048]{2,1,0:T(8,128)(2,1)}, u32[]{:S(2)}, u32[]{:S(2)}) async-start(bf16[16,72,2048]{2,1,0:T(8,128)(2,1)} %bitcast.65), calls=%async_computation.3 | async-start | bytes 9437184 | tf_op jit(solution)/shard_map/all_to_all | solution.py:78
  294.6 6.4 %copy-start.4 = (bf16[1152,384]{0,1:T(8,128)(2,1)S(1)}, bf16[1152,384]{0,1:T(8,128)(2,1)}, u32[]{:S(2)}) copy-start(bf16[1152,384]{0,1:T(8,128)(2,1)} %get-tuple-element.17) | copy-start | bytes 2654212
  301.0 6.5 %copy-start.5 = (f32[1152,384]{0,1:T(8,128)S(1)}, f32[1152,384]{0,1:T(8,128)}, u32[]{:S(2)}) copy-start(f32[1152,384]{0,1:T(8,128)} %fusion.13) | copy-start | bytes 5308420
  301.0 6.5 %copy-start.6 = (f32[1152,384]{0,1:T(8,128)S(1)}, f32[1152,384]{0,1:T(8,128)}, u32[]{:S(2)}) copy-start(f32[1152,384]{0,1:T(8,128)} %fusion.16) | copy-start | bytes 5308420
where the time goes:
time: 421 us; the launch traced here: 417 us
  waiting for transfers between devices  249 us (59%)
  local copies, waits for them, and re-layouts  78.3 us (19%)
  matrix products  46.5 us (11%)
  starting transfers between devices  30.2 us (7%)
  other arithmetic  11.4 us (3%)
    all_to_all x1, waiting for transfers between devices, local(): lax.all_to_all(send_cotangent, 'ep', split_axis=0, concat_axis=0, tiled=T...  91.6 us
    all_to_all x1, waiting for transfers between devices, local(): lax.all_to_all(send_rows, 'ep', split_axis=0, concat_axis=0, tiled=True)  80 us
    all_to_all x1, waiting for transfers between devices, local(): lax.all_to_all(grad_rows.reshape(peers, count, model_width), 'ep', split_...  77.2 us
    scatter x2, local copies, waits for them, and re-layouts, local(): jnp.zeros((total_rows, model_width), jnp.bfloat16).at[target]  47.1 us
    dot_general x3, matrix products, contract_first(): lax.dot_general(left, right, (((0,), (0,)), ((), ())), preferred_element_...  18.6 us
    dot_general x3, matrix products, contract_last(): lax.dot_general(left, right, (((1,), (1,)), ((), ())), preferred_element_...  16.1 us
    gather x1, local copies, waits for them, and re-layouts, local(): back_flat[target].astype(jnp.float32).reshape(tok_rows, choose, model_width)  12 us
  transfers between devices with their start and end apart: 5, of which 3 were waited for; matrix products, arithmetic and copies ran while one was open for 22% of the time, Pallas kernels for 0%

commit v1 on v0

--- a/solution.py
+++ b/solution.py
@@ -105,9 +105,36 @@
     return (grad_tokens, grad_routing, grad_gate, grad_up, grad_down)
 
 
+def dense_local(tokens, cotangent, expert_ids, routing, gate_proj, up_proj, down_proj):
+    peers = lax.axis_size("ep")
+    tok_rows, model_width = tokens.shape
+    experts = jnp.arange(peers, dtype=jnp.int32)
+    chosen = expert_ids[:, None, :] == experts[None, :, None]
+    weight = jnp.sum(
+        jnp.where(chosen, routing.astype(jnp.float32)[:, None, :], 0.0), axis=2
+    ).astype(jnp.bfloat16)
+    weight_in = lax.all_to_all(weight.T, "ep", split_axis=0, concat_axis=0, tiled=True)
+    rows_in = lax.all_gather(tokens, "ep", axis=0, tiled=True)
+    cotangent_in = lax.all_gather(cotangent, "ep", axis=0, tiled=True)
+    grad_rows, delta_prob, gate_grad, up_grad, scaled_hidden = expert_rows(
+        rows_in, cotangent_in, weight_in.reshape(-1), gate_proj[0], up_proj[0], down_proj[0]
+    )
+    back_prob = lax.all_to_all(
+        delta_prob.reshape(peers, tok_rows), "ep", split_axis=0, concat_axis=0, tiled=True
+    )
+    grad_tokens = lax.psum_scatter(grad_rows, "ep", scatter_dimension=0, tiled=True)
+    grad_gate = contract_first(rows_in, gate_grad).astype(jnp.bfloat16)[None]
+    grad_up = contract_first(rows_in, up_grad).astype(jnp.bfloat16)[None]
+    grad_down = contract_first(scaled_hidden, cotangent_in).astype(jnp.bfloat16)[None]
+    grad_routing = jnp.sum(
+        jnp.where(chosen, back_prob.T.astype(jnp.float32)[:, :, None], 0.0), axis=1
+    ).astype(jnp.bfloat16)
+    return (grad_tokens, grad_routing, grad_gate, grad_up, grad_down)
+
+
 def solution(mesh):
     return jax.shard_map(
-        local,
+        dense_local if mesh.shape["ep"] <= 16 else local,
         mesh=mesh,
         in_specs=(
             P(("grp", "ep"), None),

time: 421 us -> 326 us (0.77)
  the two profiles are of different devices: /device:TPU:15 before, /device:TPU:0 now
where the time goes in v1:
time: 326 us
  waiting for transfers between devices  218 us (67%)
  matrix products  69.2 us (21%)
  between operations  13.8 us (4%)
  blocking collectives  8.97 us (3%)
  local copies, waits for them, and re-layouts  6.31 us (2%)
  other arithmetic  5.3 us (2%)
  starting transfers between devices  3.59 us (1%)
    all_gather x1, waiting for transfers between devices, dense_local(): rows_in = lax.all_gather(tokens, 'ep', axis=0, tiled=True)  79.1 us
    reduce_scatter x1, waiting for transfers between devices, dense_local(): lax.psum_scatter(grad_rows, 'ep', scatter_dimension=0, tiled=True)  70.4 us
    all_gather x1, waiting for transfers between devices, dense_local(): cotangent_in = lax.all_gather(cotangent, 'ep', axis=0, tiled=True)  61.3 us
    dot_general x3, matrix products, contract_last(): lax.dot_general(left, right, (((1,), (1,)), ((), ())), preferred_element_...  29.3 us
    dot_general x3, matrix products, contract_first(): lax.dot_general(left, right, (((0,), (0,)), ((), ())), preferred_element_...  26 us
    all_to_all x1, blocking collectives, dense_local(): lax.all_to_all(weight.T, 'ep', split_axis=0, concat_axis=0, tiled=True)  8.97 us
    dot_general x1, matrix products, expert_rows(): gate_pre = jnp.dot(rows_in, gate_w, preferred_element_type=jnp.float32)  8.71 us
  transfers between devices with their start and end apart: 4, of which 4 were waited for; matrix products, arithmetic and copies ran while one was open for 14% of the time, Pallas kernels for 0%

profile of v1, /device:TPU:0, one launch (start us, length us, event | category | flops | bytes accessed | tf_op | source)
XLA Modules:
  0.0 325.7 jit_solution(15984897260874045570)
XLA Ops:
  7.2 0.7 all-gather.5.cloned.1.call-update
  7.9 0.0 all-gather.3.cloned.1.call-start
  8.0 0.7 all-gather.3.cloned.1.call-update
  8.7 79.1 %all-gather.5.cloned.1.call-done = bf16[2048,2048]{1,0:T(8,128)(2,1)} async-done(((bf16[128,2048]{1,0:T(8,128)(2,1)}), bf16[2048,2048]{1,0:T(8,128)(2,1)}) %all-gather.5.cloned.1.call-update) | async-done | bytes 8388624 | tf_op jit(solution)/shard_map/all_gather | solution.py:117
  87.8 8.7 %fusion.6 = f32[2048,384]{0,1:T(8,128)} fusion(bf16[2048,2048]{1,0:T(8,128)(2,1)} %all-gather.5.cloned.1.call-done, bf16[1,2048,384]{2,1,0:T(8,128)(2,1)S(1)} %copy-done), kind=kOutput, calls=%fused_computation.15 | convolution fusion | flops 3221225472 | bytes 13107200 | tf_op jit(solution)/shard_map/dot_general | solution.py:20
  96.5 5.3 %fusion.9 = f32[2048,384]{0,1:T(8,128)} fusion(bf16[2048,2048]{1,0:T(8,128)(2,1)S(1)} %copy-done.8, bf16[1,2048,384]{2,1,0:T(8,128)(2,1)S(1)} %copy-done.4), kind=kOutput, calls=%fused_computation.18 | convolution fusion | flops 3221225472 | bytes 13107200 | tf_op jit(solution)/shard_map/dot_general | solution.py:21
  101.8 61.3 %all-gather.3.cloned.1.call-done = bf16[2048,2048]{1,0:T(8,128)(2,1)} async-done(((bf16[128,2048]{1,0:T(8,128)(2,1)}), bf16[2048,2048]{1,0:T(8,128)(2,1)}) %all-gather.3.cloned.1.call-update) | async-done | bytes 8388624 | tf_op jit(solution)/shard_map/all_gather | solution.py:118
  163.2 10.9 %multiply_reduce_fusion = (bf16[2048]{0:T(1024)(128)(2,1)S(1)}, f32[2048,384]{0,1:T(8,128)}) fusion(f32[2048,384]{0,1:T(8,128)} %fusion.9, f32[2048,384]{0,1:T(8,128)} %fusion.6, bf16[2048,2048]{1,0:T(8,128)(2,1)} %all-gather.3.cloned.1.call-done, bf16[1,384,2048]{2,1,0:T(8,128)(2,1)} %param.13), kind=kOutput, calls=%fused_computation.2 | convolution fusion | flops 3226728448 | bytes 19402752 | tf_op jit(solution)/shard_map/dot_general | solution.py:8
  174.0 0.6 copy.38
  174.6 3.5 %all-to-all-start.1 = ((bf16[16,1,128]{2,1,0:T(2,128)(2,1)}), bf16[16,1,128]{2,1,0:T(2,128)(2,1)S(1)}, u32[]{:S(2)}, u32[]{:S(2)}) async-start(bf16[16,1,128]{2,1,0:T(2,128)(2,1)} %copy.38), calls=%async_computation.2 | async-start | bytes 16384 | tf_op jit(solution)/shard_map/all_to_all | solution.py:122
  178.1 0.0 reduce-scatter.2.cloned.1.call-start
  178.2 6.2 %all-to-all-done.1 = bf16[16,1,128]{2,1,0:T(2,128)(2,1)S(1)} async-done(((bf16[16,1,128]{2,1,0:T(2,128)(2,1)}), bf16[16,1,128]{2,1,0:T(2,128)(2,1)S(1)}, u32[]{:S(2)}, u32[]{:S(2)}) %all-to-all-start.1) | async-done | bytes 4128 | tf_op jit(solution)/shard_map/all_to_all | solution.py:122
  184.4 0.6 select_reduce_fusion
  185.1 9.0 %all_to_all.15 = bf16[16,1,128]{2,1,0:T(2,128)(2,1)S(1)} all-to-all(bf16[16,1,128]{2,1,0:T(2,128)(2,1)S(1)} %copy.36), channel_id=1, replica_groups=mesh['grp'=2,'ep'=16] {'ep'}, dimensions={0} | all-to-all | bytes 8192 | tf_op jit(solution)/shard_map/all_to_all | solution.py:116
  194.0 4.7 %multiply_convert_fusion.1 = (bf16[2048,384]{0,1:T(8,128)(2,1)S(1)}, bf16[2048,384]{0,1:T(8,128)(2,1)S(1)}) fusion(f32[2048,384]{0,1:T(8,128)} %get-tuple-element.35, f32[2048]{0:T(1024)S(1)} %bitcast_convert_fusion, f32[2048,384]{0,1:T(8,128)} %fusion.6, f32[2048,384]{0,1:T(8,128)} %fusion.9), kind=kLoop, calls=%fused_computation.3 | loop fusion | flops 11010048 | bytes 12591104 | tf_op jit(solution)/shard_map/convert_element_type | solution.py:29
  198.7 8.2 %fusion.4 = f32[2048,2048]{1,0:T(8,128)} fusion(bf16[2048,384]{0,1:T(8,128)(2,1)S(1)} %get-tuple-element.33, bf16[1,2048,384]{2,1,0:T(8,128)(2,1)S(1)} %copy-done), kind=kOutput, calls=%fused_computation.13 | convolution fusion | flops 3221225472 | bytes 19922944 | tf_op jit(solution)/shard_map/dot_general | solution.py:8
  206.9 10.2 %add_convert_fusion = bf16[2048,2048]{1,0:T(8,128)(2,1)} fusion(f32[2048,2048]{1,0:T(8,128)} %fusion.4, bf16[2048,384]{0,1:T(8,128)(2,1)S(1)} %get-tuple-element.32, bf16[1,2048,384]{2,1,0:T(8,128)(2,1)S(1)} %copy-done.5), kind=kOutput, calls=%fused_computation | convolution fusion | flops 3229614080 | bytes 28311552 | tf_op jit(solution)/shard_map/dot_general | solution.py:8
  217.2 1.4 copy-done.3
  218.5 8.4 %fusion.1 = bf16[1,2048,384]{1,2,0:T(8,128)(2,1)} fusion(bf16[2048,384]{0,1:T(8,128)(2,1)S(1)} %copy-done.3, bf16[2048,2048]{1,0:T(8,128)(2,1)} %all-gather.5.cloned.1.call-done), kind=kOutput, calls=%fused_computation.10 | convolution fusion | flops 3222011904 | bytes 11534336 | tf_op jit(solution)/shard_map/dot_general | solution.py:14
  226.9 2.7 copy.39
  229.6 7.6 %fusion.2 = bf16[1,2048,384]{1,2,0:T(8,128)(2,1)S(1)} fusion(bf16[2048,384]{0,1:T(8,128)(2,1)S(1)} %get-tuple-element.32, bf16[2048,2048]{1,0:T(8,128)(2,1)} %all-gather.5.cloned.1.call-done), kind=kOutput, calls=%fused_computation.11 | convolution fusion | flops 3222011904 | bytes 11534336 | tf_op jit(solution)/shard_map/dot_general | solution.py:14
  237.2 1.6 copy.40
  238.8 10.0 %fusion.3 = bf16[1,384,2048]{2,1,0:T(8,128)(2,1)} fusion(bf16[2048,2048]{1,0:T(8,128)(2,1)} %all-gather.3.cloned.1.call-done, f32[2048]{0:T(1024)S(1)} %bitcast_convert_fusion, f32[2048,384]{0,1:T(8,128)} %fusion.9, f32[2048,384]{0,1:T(8,128)} %fusion.6), kind=kOutput, calls=%fused_computation.12 | convolution fusion | flops 3227516928 | bytes 16261120 | tf_op jit(solution)/shard_map/dot_general | solution.py:14
  248.8 70.4 %reduce-scatter.2.cloned.1.call-done = bf16[128,2048]{1,0:T(8,128)(2,1)} async-done(((bf16[2048,2048]{1,0:T(8,128)(2,1)}), bf16[128,2048]{1,0:T(8,128)(2,1)}) %reduce-scatter.2.cloned.1.call-update) | async-done | bytes 524304 | tf_op jit(solution)/shard_map/reduce_scatter | solution.py:125
  (23 shorter events, 0.1 us)
Async XLA Ops:
  7.2 80.6 %copy-start = (bf16[1,2048,384]{2,1,0:T(8,128)(2,1)S(1)}, bf16[1,2048,384]{2,1,0:T(8,128)(2,1)}, u32[]{:S(2)}) copy-start(bf16[1,2048,384]{2,1,0:T(8,128)(2,1)} %param.11) | copy-start | bytes 4718596
  7.2 80.6 %all-gather.5.cloned.1.call-start = ((), (), s32[]{:S(2)}) async-start(), calls=%async_computation.4 | async-start | bytes 8912896 | tf_op jit(solution)/shard_map/all_gather | solution.py:117
  7.9 155.2 %all-gather.3.cloned.1.call-start = ((), (), s32[]{:S(2)}) async-start(), calls=%async_computation.3 | async-start | bytes 8912896 | tf_op jit(solution)/shard_map/all_gather | solution.py:118
  8.7 87.9 %copy-start.4 = (bf16[1,2048,384]{2,1,0:T(8,128)(2,1)S(1)}, bf16[1,2048,384]{2,1,0:T(8,128)(2,1)}, u32[]{:S(2)}) copy-start(bf16[1,2048,384]{2,1,0:T(8,128)(2,1)} %param.12) | copy-start | bytes 4718596
  87.8 8.7 %copy-start.8 = (bf16[2048,2048]{1,0:T(8,128)(2,1)S(1)}, bf16[2048,2048]{1,0:T(8,128)(2,1)}, u32[]{:S(2)}) copy-start(bf16[2048,2048]{1,0:T(8,128)(2,1)} %all-gather.5.cloned.1.call-done) | copy-start | bytes 25165828
  101.8 76.4 %copy-start.7 = (bf16[128,8]{0,1:T(8,128)(2,1)S(1)}, bf16[128,8]{0,1:T(8,128)(2,1)}, u32[]{:S(2)}) copy-start(bf16[128,8]{0,1:T(8,128)(2,1)} %param.10) | copy-start | bytes 6148
  101.8 82.6 %copy-start.6 = (s32[128,8]{0,1:T(8,128)S(1)}, s32[128,8]{0,1:T(8,128)}, u32[]{:S(2)}) copy-start(s32[128,8]{0,1:T(8,128)} %param.9) | copy-start | bytes 12292
  174.6 9.8 %all-to-all-start.1 = ((bf16[16,1,128]{2,1,0:T(2,128)(2,1)}), bf16[16,1,128]{2,1,0:T(2,128)(2,1)S(1)}, u32[]{:S(2)}, u32[]{:S(2)}) async-start(bf16[16,1,128]{2,1,0:T(2,128)(2,1)} %copy.38), calls=%async_computation.2 | async-start | bytes 16384 | tf_op jit(solution)/shard_map/all_to_all | solution.py:122
  178.1 141.0 %reduce-scatter.2.cloned.1.call-start = ((), (), s32[]{:S(2)}) async-start(), calls=%async_computation.5 | async-start | bytes 8912896 | tf_op jit(solution)/shard_map/reduce_scatter | solution.py:125
  198.7 8.2 %copy-start.2 = (bf16[2048,384]{0,1:T(8,128)(2,1)}, bf16[2048,384]{0,1:T(8,128)(2,1)S(1)}, u32[]{:S(2)}) copy-start(bf16[2048,384]{0,1:T(8,128)(2,1)S(1)} %get-tuple-element.33) | copy-start | bytes 4718596
  198.7 8.2 %copy-start.5 = (bf16[1,2048,384]{2,1,0:T(8,128)(2,1)S(1)}, bf16[1,2048,384]{2,1,0:T(8,128)(2,1)}, u32[]{:S(2)}) copy-start(bf16[1,2048,384]{2,1,0:T(8,128)(2,1)} %param.12) | copy-start | bytes 4718596
  217.1 1.4 copy-start.3
  238.8 80.4 %copy-start.1 = (bf16[1,2048,384]{2,1,0:T(8,128)(2,1)S(1)}, bf16[1,2048,384]{2,1,0:T(8,128)(2,1)}, u32[]{:S(2)}) copy-start(bf16[1,2048,384]{2,1,0:T(8,128)(2,1)} %param.11) | copy-start | bytes 4718596
Sparse Core Ops, SparseCore 0:
  10.2 77.5 all-gather.4
  90.0 73.1 all-gather.2
  217.3 101.8 reduce-scatter.1

commit v2 on v0

--- a/solution.py
+++ b/solution.py
@@ -1,6 +1,10 @@
+import functools
+
 import jax
 import jax.numpy as jnp
 from jax import lax
+from jax.experimental import pallas as pl
+from jax.experimental.pallas import tpu as pltpu
 from jax.sharding import PartitionSpec as P
 
 
@@ -105,9 +109,468 @@
     return (grad_tokens, grad_routing, grad_gate, grad_up, grad_down)
 
 
+LANES = 128
+
+
+def pick(table, row, column):
+    value = jnp.int32(0)
+    for r, entries in enumerate(table):
+        for s, entry in enumerate(entries):
+            value = value + jnp.where((row == r) & (column == s), entry, 0)
+    return value
+
+
+def expert_kernel(
+    depth,
+    first_rows,
+    tokens_ref,
+    cotangent_ref,
+    ids_ref,
+    routing_ref,
+    gate_hbm,
+    up_hbm,
+    down_hbm,
+    grad_tokens_ref,
+    grad_routing_ref,
+    grad_pair_ref,
+    grad_down_ref,
+    rows_all,
+    partial,
+    core_in,
+    side_in,
+    rise_in,
+    fall_in,
+    pair_t,
+    hidden_t,
+    gate_w,
+    up_w,
+    down_w,
+    local_sem,
+    gather_send,
+    gather_recv,
+    core_send,
+    core_recv,
+    side_send,
+    side_recv,
+    chain_send,
+    chain_recv,
+):
+    block, width = tokens_ref.shape
+    hidden_width = gate_w.shape[1]
+    me = lax.axis_index("ep")
+    z, y, c = me // 4, (me // 2) % 2, me % 2
+    sibling = z * 4 + y * 2 + (1 - c)
+    side = z * 4 + (1 - y) * 2 + c
+    above, below = me + 4, me - 4
+    near = [sorted(range(depth), key=lambda o, r=r: (abs(o - r), o)) for r in range(depth)]
+    chain = [
+        list(range(r + 1, depth)) + list(range(r - 1, -1, -1))
+        if r < depth // 2
+        else list(range(r - 1, -1, -1)) + list(range(r + 1, depth))
+        for r in range(depth)
+    ]
+    parts = ((0, first_rows), (first_rows, block - first_rows))
+
+    def at_rows(o, n=1):
+        return pl.ds(pl.multiple_of(o * block, block), n * block)
+
+    def local_copies():
+        mine = at_rows(me)
+        return (
+            pltpu.make_async_copy(tokens_ref, rows_all.at[mine, 0:width], local_sem.at[0]),
+            pltpu.make_async_copy(
+                cotangent_ref, rows_all.at[mine, width : 2 * width], local_sem.at[1]
+            ),
+            pltpu.make_async_copy(gate_hbm, gate_w, local_sem.at[2]),
+            pltpu.make_async_copy(up_hbm, up_w, local_sem.at[3]),
+            pltpu.make_async_copy(down_hbm, down_w, local_sem.at[4]),
+        )
+
+    def gather_copy(kind, o, way, target):
+        start, size = parts[kind]
+        where = rows_all.at[pl.ds(pl.multiple_of(o * block + start, 16), size), :]
+        return pltpu.make_async_remote_copy(
+            src_ref=where,
+            dst_ref=where,
+            send_sem=gather_send.at[kind, way, o],
+            recv_sem=gather_recv.at[kind, o],
+            device_id={"ep": target},
+            device_id_type=pl.DeviceIdType.MESH,
+        )
+
+    def send_along(kind, zo, o):
+        @pl.when((zo <= z) & (z < depth - 1))
+        def _():
+            gather_copy(kind, o, 0, above).start()
+
+        @pl.when((zo >= z) & (z > 0))
+        def _():
+            gather_copy(kind, o, 1, below).start()
+
+    def arrive(kind, o):
+        gather_copy(kind, o, 3, sibling).wait_recv()
+
+    def forward(s):
+        zo = pick(near, z, s)
+        own = zo * 4 + y * 2 + c
+        other = zo * 4 + (1 - y) * 2 + c
+
+        @pl.when(s > 0)
+        def _():
+            arrive(0, own)
+
+        send_along(0, zo, own)
+        gather_copy(0, own, 2, side).start()
+
+        @pl.when(s > 0)
+        def _():
+            arrive(1, own)
+
+        send_along(1, zo, own)
+
+        @pl.when(s == 0)
+        def _():
+            gather_copy(1, own, 2, side).start()
+
+        gather_copy(0, own, 3, sibling).start()
+        gather_copy(1, own, 3, sibling).start()
+        arrive(1, other)
+        send_along(1, zo, other)
+        gather_copy(1, other, 3, sibling).start()
+
+    def core_copy(zo, yo):
+        return pltpu.make_async_remote_copy(
+            src_ref=partial.at[at_rows(zo * 4 + yo * 2 + (1 - c)), :],
+            dst_ref=core_in.at[at_rows(zo * 2 + yo), :],
+            send_sem=core_send.at[zo * 2 + yo],
+            recv_sem=core_recv.at[zo * 2 + yo],
+            device_id={"ep": sibling},
+            device_id_type=pl.DeviceIdType.MESH,
+        )
+
+    def side_copy(zo):
+        return pltpu.make_async_remote_copy(
+            src_ref=partial.at[at_rows(zo * 4 + (1 - y) * 2 + c), :],
+            dst_ref=side_in.at[at_rows(zo), :],
+            send_sem=side_send.at[zo],
+            recv_sem=side_recv.at[zo],
+            device_id={"ep": side},
+            device_id_type=pl.DeviceIdType.MESH,
+        )
+
+    def chain_copy(zo, way, target):
+        return pltpu.make_async_remote_copy(
+            src_ref=partial.at[at_rows(zo * 4 + y * 2 + c), :],
+            dst_ref=(rise_in if way == 0 else fall_in).at[at_rows(zo), :],
+            send_sem=chain_send.at[way, zo],
+            recv_sem=chain_recv.at[way, zo],
+            device_id={"ep": target},
+            device_id_type=pl.DeviceIdType.MESH,
+        )
+
+    def add_into(o, source, at):
+        total = partial[at_rows(o), :].astype(jnp.float32) + source[at_rows(at), :].astype(
+            jnp.float32
+        )
+        partial[at_rows(o), :] = total.astype(jnp.bfloat16)
+
+    def compute(s):
+        zo = pick(near, z, s)
+        other = zo * 4 + (1 - y) * 2 + c
+        arrive(0, other)
+        gather_copy(0, other, 3, sibling).start()
+        for kind in (0, 1):
+            for yo in (0, 1):
+                arrive(kind, zo * 4 + yo * 2 + (1 - c))
+
+        @pl.when(s == 0)
+        def _():
+            for copy in local_copies()[2:]:
+                copy.wait()
+
+        @pl.loop(0, 2)
+        def _(yo):
+            start = pl.multiple_of((zo * 4 + yo * 2) * block, 2 * block)
+            rows = pl.ds(start, 2 * block)
+            lane = lax.broadcasted_iota(jnp.int32, (2 * block, LANES), 1)
+            x = rows_all[rows, 0:width]
+            gate_pre = jnp.dot(x, gate_w[...], preferred_element_type=jnp.float32)
+            up_pre = jnp.dot(x, up_w[...], preferred_element_type=jnp.float32)
+            hidden_raw = contract_last(rows_all[rows, width : 2 * width], down_w[...])
+            weights = rows_all[rows, 2 * width : 2 * width + LANES].astype(jnp.float32)
+            scale_col = jnp.sum(jnp.where(lane == me, weights, 0.0), axis=1, keepdims=True)
+            gate_sigmoid = jax.nn.sigmoid(gate_pre)
+            activated = gate_pre * gate_sigmoid
+            hidden = activated * up_pre
+            delta_prob = jnp.sum(hidden * hidden_raw, axis=1, keepdims=True)
+            partial[rows, width : width + LANES] = jnp.where(lane == me, delta_prob, 0.0).astype(
+                jnp.bfloat16
+            )
+            hidden_grad = scale_col * hidden_raw
+            up_grad = hidden_grad * activated
+            gate_grad = (
+                hidden_grad * up_pre * gate_sigmoid * (1.0 + gate_pre * (1.0 - gate_sigmoid))
+            )
+            pair_t[0:hidden_width, rows] = gate_grad.T.astype(jnp.bfloat16)
+            pair_t[hidden_width : 2 * hidden_width, rows] = up_grad.T.astype(jnp.bfloat16)
+            hidden_t[:, rows] = (scale_col * hidden).T.astype(jnp.bfloat16)
+            up_grad = up_grad.astype(jnp.bfloat16)
+            gate_grad = gate_grad.astype(jnp.bfloat16)
+            for tile in range(0, width, 512):
+                span = slice(tile, tile + 512)
+                partial[rows, span] = (
+                    contract_last(gate_grad, gate_w[span, :])
+                    + contract_last(up_grad, up_w[span, :])
+                ).astype(jnp.bfloat16)
+            core_copy(zo, yo).start()
+
+    def sum_core(s):
+        zo = pick(near, z, s)
+        core_copy(zo, 1 - y).wait_recv()
+        add_into(zo * 4 + (1 - y) * 2 + c, core_in, zo * 2 + (1 - y))
+        side_copy(zo).start()
+        core_copy(zo, y).wait_recv()
+        add_into(zo * 4 + y * 2 + c, core_in, zo * 2 + y)
+
+    def sum_side(s):
+        zo = pick(near, z, s)
+        side_copy(zo).wait_recv()
+        add_into(zo * 4 + y * 2 + c, side_in, zo)
+
+    def sum_chain(s):
+        zo = pick(chain, z, s)
+        own = zo * 4 + y * 2 + c
+
+        @pl.when(zo > z)
+        def _():
+            @pl.when(z > 0)
+            def _():
+                chain_copy(zo, 0, above).wait_recv()
+                add_into(own, rise_in, zo)
+
+            chain_copy(zo, 0, above).start()
+
+        @pl.when(zo < z)
+        def _():
+            @pl.when(z < depth - 1)
+            def _():
+                chain_copy(zo, 1, below).wait_recv()
+                add_into(own, fall_in, zo)
+
+            chain_copy(zo, 1, below).start()
+
+    tile_width = 256
+
+    def weight_grads(low, high):
+        @pl.loop(low, high)
+        def _(tile):
+            start = pl.multiple_of(tile * tile_width, tile_width)
+            span = pl.ds(start, tile_width)
+            grad_pair_ref[:, span] = jnp.dot(
+                pair_t[...], rows_all[:, span], preferred_element_type=jnp.float32
+            ).astype(jnp.bfloat16)
+            grad_down_ref[:, span] = jnp.dot(
+                hidden_t[...],
+                rows_all[:, pl.ds(pl.multiple_of(start + width, tile_width), tile_width)],
+                preferred_element_type=jnp.float32,
+            ).astype(jnp.bfloat16)
+
+    for copy in local_copies():
+        copy.start()
+    barrier = pltpu.get_barrier_semaphore()
+    for target in (sibling, side):
+        pl.semaphore_signal(
+            barrier, inc=1, device_id={"ep": target}, device_id_type=pl.DeviceIdType.MESH
+        )
+
+    @pl.when(z < depth - 1)
+    def _():
+        pl.semaphore_signal(
+            barrier, inc=1, device_id={"ep": above}, device_id_type=pl.DeviceIdType.MESH
+        )
+
+    @pl.when(z > 0)
+    def _():
+        pl.semaphore_signal(
+            barrier, inc=1, device_id={"ep": below}, device_id_type=pl.DeviceIdType.MESH
+        )
+
+    ends = jnp.where(z > 0, 1, 0) + jnp.where(z < depth - 1, 1, 0)
+    pl.semaphore_wait(barrier, 2 + ends)
+    lane = lax.broadcasted_iota(jnp.int32, (block, LANES), 1)
+    choose = ids_ref.shape[1]
+    weights = jnp.zeros((block, LANES), jnp.float32)
+    for k in range(choose):
+        weights = weights + jnp.where(
+            lane == ids_ref[:, k : k + 1], routing_ref[:, k : k + 1].astype(jnp.float32), 0.0
+        )
+    rows_all[at_rows(me), 2 * width : 2 * width + LANES] = weights.astype(jnp.bfloat16)
+    for copy in local_copies()[:2]:
+        copy.wait()
+
+    last = depth - 1
+
+    @pl.loop(0, depth + 3)
+    def _(s):
+        @pl.when(s < depth)
+        def _():
+            forward(s)
+
+        @pl.when((s >= 1) & (s <= depth))
+        def _():
+            compute(s - 1)
+
+        @pl.when((s >= 2) & (s <= depth + 1))
+        def _():
+            sum_core(s - 2)
+
+        @pl.when(s >= 3)
+        def _():
+            sum_side(s - 3)
+
+        @pl.when(s == depth + 1)
+        def _():
+            sum_chain(0)
+            weight_grads(0, 5)
+
+    sum_chain(1)
+    weight_grads(5, 6)
+    for s in range(2, last):
+        sum_chain(s)
+    weight_grads(6, width // tile_width)
+
+    @pl.when(z > 0)
+    def _():
+        chain_copy(z, 0, above).wait_recv()
+
+    @pl.when(z == 0)
+    def _():
+        rise_in[at_rows(z), :] = jnp.zeros((block, width + LANES), jnp.bfloat16)
+
+    @pl.when(z < depth - 1)
+    def _():
+        chain_copy(z, 1, below).wait_recv()
+
+    @pl.when(z == depth - 1)
+    def _():
+        fall_in[at_rows(z), :] = jnp.zeros((block, width + LANES), jnp.bfloat16)
+
+    total = (
+        partial[at_rows(me), :].astype(jnp.float32)
+        + rise_in[at_rows(z), :].astype(jnp.float32)
+        + fall_in[at_rows(z), :].astype(jnp.float32)
+    )
+    grad_tokens_ref[...] = total[:, :width].astype(jnp.bfloat16)
+    probs = total[:, width:]
+    found = jnp.zeros((block, LANES), jnp.float32)
+    for k in range(choose):
+        value = jnp.sum(
+            jnp.where(lane == ids_ref[:, k : k + 1], probs, 0.0), axis=1, keepdims=True
+        )
+        found = found + jnp.where(lane == k, value, 0.0)
+    grad_routing_ref[...] = found.astype(jnp.bfloat16)
+
+    @pl.loop(0, depth)
+    def _(zo):
+        own = zo * 4 + y * 2 + c
+        other = zo * 4 + (1 - y) * 2 + c
+        for kind, o in ((0, own), (1, own), (1, other)):
+            @pl.when((zo <= z) & (z < depth - 1))
+            def _(kind=kind, o=o):
+                gather_copy(kind, o, 0, above).wait_send()
+
+            @pl.when((zo >= z) & (z > 0))
+            def _(kind=kind, o=o):
+                gather_copy(kind, o, 1, below).wait_send()
+
+        gather_copy(0, own, 2, side).wait_send()
+
+        @pl.when(zo == z)
+        def _():
+            gather_copy(1, own, 2, side).wait_send()
+
+        for kind in (0, 1):
+            for o in (own, other):
+                gather_copy(kind, o, 3, sibling).wait_send()
+        core_copy(zo, 0).wait_send()
+        core_copy(zo, 1).wait_send()
+        side_copy(zo).wait_send()
+
+        @pl.when(zo > z)
+        def _():
+            chain_copy(zo, 0, above).wait_send()
+
+        @pl.when(zo < z)
+        def _():
+            chain_copy(zo, 1, below).wait_send()
+
+
+def dense_local(tokens, cotangent, expert_ids, routing, gate_proj, up_proj, down_proj):
+    peers = lax.axis_size("ep")
+    depth = peers // 4
+    block, width = tokens.shape
+    choose = expert_ids.shape[1]
+    hidden_width = gate_proj.shape[2]
+    total = peers * block
+    first_rows = block * 5 // 8
+    bf16 = jnp.bfloat16
+    vmem = pl.BlockSpec(memory_space=pltpu.VMEM)
+    anywhere = pl.BlockSpec(memory_space=pl.ANY)
+    dma = pltpu.SemaphoreType.DMA
+    grad_tokens, grad_routing, grad_pair, grad_down = pl.pallas_call(
+        functools.partial(expert_kernel, depth, first_rows),
+        out_shape=(
+            jax.ShapeDtypeStruct((block, width), bf16),
+            jax.ShapeDtypeStruct((block, LANES), bf16),
+            jax.ShapeDtypeStruct((2 * hidden_width, width), bf16),
+            jax.ShapeDtypeStruct((hidden_width, width), bf16),
+        ),
+        in_specs=[anywhere, anywhere, vmem, vmem, anywhere, anywhere, anywhere],
+        out_specs=(vmem, vmem, vmem, vmem),
+        scratch_shapes=[
+            pltpu.VMEM((total, 2 * width + LANES), bf16),
+            pltpu.VMEM((total, width + LANES), bf16),
+            pltpu.VMEM((total // 2, width + LANES), bf16),
+            pltpu.VMEM((total // 4, width + LANES), bf16),
+            pltpu.VMEM((total // 4, width + LANES), bf16),
+            pltpu.VMEM((total // 4, width + LANES), bf16),
+            pltpu.VMEM((2 * hidden_width, total), bf16),
+            pltpu.VMEM((hidden_width, total), bf16),
+            pltpu.VMEM((width, hidden_width), bf16),
+            pltpu.VMEM((width, hidden_width), bf16),
+            pltpu.VMEM((hidden_width, width), bf16),
+            dma((5,)),
+            dma((2, 4, peers)),
+            dma((2, peers)),
+            dma((2 * depth,)),
+            dma((2 * depth,)),
+            dma((depth,)),
+            dma((depth,)),
+            dma((2, depth)),
+            dma((2, depth)),
+        ],
+        compiler_params=pltpu.CompilerParams(
+            collective_id=0, has_side_effects=True, vmem_limit_bytes=62 << 20
+        ),
+        cost_estimate=pl.CostEstimate(
+            flops=16 * total * width * hidden_width,
+            bytes_accessed=20 * width * hidden_width,
+            transcendentals=total * hidden_width,
+        ),
+    )(tokens, cotangent, expert_ids, routing, gate_proj[0], up_proj[0], down_proj[0])
+    grad_pair = grad_pair.reshape(2, hidden_width, width)
+    return (
+        grad_tokens,
+        grad_routing[:, :choose],
+        grad_pair[:1].transpose(0, 2, 1),
+        grad_pair[1:].transpose(0, 2, 1),
+        grad_down[None],
+    )
+
+
 def solution(mesh):
     return jax.shard_map(
-        local,
+        dense_local if mesh.shape["ep"] == 16 else local,
         mesh=mesh,
         in_specs=(
             P(("grp", "ep"), None),

time: 421 us -> 221 us (0.52)
  the two profiles are of different devices: /device:TPU:15 before, /device:TPU:0 now
where the time goes in v2:
time: 221 us
  Pallas kernels  207 us (94%)
  local copies, waits for them, and re-layouts  12.5 us (6%)
    pallas_call x1, Pallas kernels, dense_local(): pl.pallas_call(functools.partial(expert_kernel, depth, first_rows), out_s...  207 us
    unnamed x9, local copies, waits for them, and re-layouts  10.4 us

profile of v2, /device:TPU:0, one launch (start us, length us, event | category | flops | bytes accessed | tf_op | source)
XLA Modules:
  0.0 220.5 jit_solution(8954549061230087111)
XLA Ops:
  0.6 1.4 copy.13.routing_ref
  2.0 1.4 copy.12.ids_ref
  3.4 207.4 %shard_map.110 = (bf16[128,2048]{1,0:T(8,128)(2,1)}, bf16[128,128]{1,0:T(8,128)(2,1)}, bf16[768,2048]{1,0:T(8,128)(2,1)}, bf16[384,2048]{1,0:T(8,128)(2,1)}) custom-call(bf16[128,2048]{1,0:T(8,128)(2,1)} %tokens_ref.1, bf16[128,2048]{1,0:T(8,128)(2,1)} %cotangent_ref.1, s32[128,8]{1,0:T(8,128)} %copy.12.ids_ref, bf16[128,8]{1,0:T(8,128)(2,1)} %copy.13.routing_ref, ...), custom_call_target="tpu_custom_call" | custom-call | flops 25769803776 | bytes 15728640 | tf_op jit(solution)/shard_map/pallas_call | solution.py:520
  210.9 1.4 copy.14
  212.3 2.1 slice_bitcast_fusion
  214.4 1.6 copy.16
  215.9 0.0 copy-start
  215.9 1.6 copy.15
  217.5 1.9 copy.19
  219.4 0.0 copy-done
  219.4 1.1 copy.20
Async XLA Ops:
  215.9 3.4 %copy-start = (bf16[384,2048]{1,0:T(8,128)(2,1)S(1)}, bf16[384,2048]{1,0:T(8,128)(2,1)}, u32[]{:S(2)}) copy-start(bf16[384,2048]{1,0:T(8,128)(2,1)} %get-tuple-element.12) | copy-start | bytes 4718596

commit v3 on v2

--- a/solution.py
+++ b/solution.py
@@ -258,12 +258,16 @@
             device_id_type=pl.DeviceIdType.MESH,
         )
 
-    def chain_copy(zo, way, target):
+    def half_rows(o, half):
+        start = o * block + half * (block // 2)
+        return pl.ds(pl.multiple_of(start, block // 2), block // 2)
+
+    def chain_copy(zo, way, target, half):
         return pltpu.make_async_remote_copy(
-            src_ref=partial.at[at_rows(zo * 4 + y * 2 + c), :],
-            dst_ref=(rise_in if way == 0 else fall_in).at[at_rows(zo), :],
-            send_sem=chain_send.at[way, zo],
-            recv_sem=chain_recv.at[way, zo],
+            src_ref=partial.at[half_rows(zo * 4 + y * 2 + c, half), :],
+            dst_ref=(rise_in if way == 0 else fall_in).at[half_rows(zo, half), :],
+            send_sem=chain_send.at[way, zo, half],
+            recv_sem=chain_recv.at[way, zo, half],
             device_id={"ep": target},
             device_id_type=pl.DeviceIdType.MESH,
         )
@@ -341,23 +345,27 @@
         zo = pick(chain, z, s)
         own = zo * 4 + y * 2 + c
 
+        def pass_on(way, target, inner, source):
+            @pl.loop(0, 2)
+            def _(half):
+                @pl.when(inner)
+                def _():
+                    chain_copy(zo, way, target, half).wait_recv()
+                    rows = half_rows(own, half)
+                    total = partial[rows, :].astype(jnp.float32) + source[
+                        half_rows(zo, half), :
+                    ].astype(jnp.float32)
+                    partial[rows, :] = total.astype(jnp.bfloat16)
+
+                chain_copy(zo, way, target, half).start()
+
         @pl.when(zo > z)
         def _():
-            @pl.when(z > 0)
-            def _():
-                chain_copy(zo, 0, above).wait_recv()
-                add_into(own, rise_in, zo)
-
-            chain_copy(zo, 0, above).start()
+            pass_on(0, above, z > 0, rise_in)
 
         @pl.when(zo < z)
         def _():
-            @pl.when(z < depth - 1)
-            def _():
-                chain_copy(zo, 1, below).wait_recv()
-                add_into(own, fall_in, zo)
-
-            chain_copy(zo, 1, below).start()
+            pass_on(1, below, z < depth - 1, fall_in)
 
     tile_width = 256
 
@@ -408,9 +416,10 @@
     for copy in local_copies()[:2]:
         copy.wait()
 
+    edge = (z == 0) | (z == depth - 1)
     last = depth - 1
 
-    @pl.loop(0, depth + 3)
+    @pl.loop(0, depth + 2)
     def _(s):
         @pl.when(s < depth)
         def _():
@@ -419,29 +428,36 @@
         @pl.when((s >= 1) & (s <= depth))
         def _():
             compute(s - 1)
-
-        @pl.when((s >= 2) & (s <= depth + 1))
-        def _():
-            sum_core(s - 2)
-
-        @pl.when(s >= 3)
-        def _():
-            sum_side(s - 3)
-
-        @pl.when(s == depth + 1)
+            sum_core(s - 1)
+
+        @pl.when(s == depth)
+        def _():
+            weight_grads(0, 4)
+
+        @pl.when(s >= 2)
+        def _():
+            sum_side(s - 2)
+
+        @pl.when((s >= 3) & edge)
+        def _():
+            sum_chain(s - 3)
+
+        @pl.when((s == depth) & (z > 0) & (z < last))
         def _():
             sum_chain(0)
-            weight_grads(0, 5)
-
-    sum_chain(1)
-    weight_grads(5, 6)
-    for s in range(2, last):
-        sum_chain(s)
-    weight_grads(6, width // tile_width)
+
+    @pl.when((z > 0) & (z < last))
+    def _():
+        @pl.loop(1, last)
+        def _(s):
+            sum_chain(s)
+
+    weight_grads(4, width // tile_width)
 
     @pl.when(z > 0)
     def _():
-        chain_copy(z, 0, above).wait_recv()
+        chain_copy(z, 0, above, 0).wait_recv()
+        chain_copy(z, 0, above, 1).wait_recv()
 
     @pl.when(z == 0)
     def _():
@@ -449,7 +465,8 @@
 
     @pl.when(z < depth - 1)
     def _():
-        chain_copy(z, 1, below).wait_recv()
+        chain_copy(z, 1, below, 0).wait_recv()
+        chain_copy(z, 1, below, 1).wait_recv()
 
     @pl.when(z == depth - 1)
     def _():
@@ -498,11 +515,13 @@
 
         @pl.when(zo > z)
         def _():
-            chain_copy(zo, 0, above).wait_send()
+            chain_copy(zo, 0, above, 0).wait_send()
+            chain_copy(zo, 0, above, 1).wait_send()
 
         @pl.when(zo < z)
         def _():
-            chain_copy(zo, 1, below).wait_send()
+            chain_copy(zo, 1, below, 0).wait_send()
+            chain_copy(zo, 1, below, 1).wait_send()
 
 
 def dense_local(tokens, cotangent, expert_ids, routing, gate_proj, up_proj, down_proj):
@@ -512,7 +531,7 @@
     choose = expert_ids.shape[1]
     hidden_width = gate_proj.shape[2]
     total = peers * block
-    first_rows = block * 5 // 8
+    first_rows = block * 6 // 8
     bf16 = jnp.bfloat16
     vmem = pl.BlockSpec(memory_space=pltpu.VMEM)
     anywhere = pl.BlockSpec(memory_space=pl.ANY)
@@ -546,8 +565,8 @@
             dma((2 * depth,)),
             dma((depth,)),
             dma((depth,)),
-            dma((2, depth)),
-            dma((2, depth)),
+            dma((2, depth, 2)),
+            dma((2, depth, 2)),
         ],
         compiler_params=pltpu.CompilerParams(
             collective_id=0, has_side_effects=True, vmem_limit_bytes=62 << 20

time: 221 us -> 191 us (0.86)
  Pallas kernels: 207 us -> 177 us
    pallas_call x1, Pallas kernels: 207 us -> 177 us  [dense_local(): pl.pallas_call(functools.partial(expert_kernel, depth, first_rows), out_s...]
where the time goes in v3:
time: 191 us; the launch traced here: 190 us
  Pallas kernels  177 us (93%)
  local copies, waits for them, and re-layouts  12.5 us (7%)
    pallas_call x1, Pallas kernels, dense_local(): pl.pallas_call(functools.partial(expert_kernel, depth, first_rows), out_s...  177 us
    unnamed x9, local copies, waits for them, and re-layouts  10.4 us

profile of v3, /device:TPU:0, one launch (start us, length us, event | category | flops | bytes accessed | tf_op | source)
XLA Modules:
  0.0 189.9 jit_solution(14764179502352050525)
XLA Ops:
  0.6 1.4 copy.13.routing_ref
  2.0 1.4 copy.12.ids_ref
  3.4 176.8 %shard_map.110 = (bf16[128,2048]{1,0:T(8,128)(2,1)}, bf16[128,128]{1,0:T(8,128)(2,1)}, bf16[768,2048]{1,0:T(8,128)(2,1)}, bf16[384,2048]{1,0:T(8,128)(2,1)}) custom-call(bf16[128,2048]{1,0:T(8,128)(2,1)} %tokens_ref.1, bf16[128,2048]{1,0:T(8,128)(2,1)} %cotangent_ref.1, s32[128,8]{1,0:T(8,128)} %copy.12.ids_ref, bf16[128,8]{1,0:T(8,128)(2,1)} %copy.13.routing_ref, ...), custom_call_target="tpu_custom_call" | custom-call | flops 25769803776 | bytes 15728640 | tf_op jit(solution)/shard_map/pallas_call | solution.py:539
  180.2 1.4 copy.14
  181.6 2.1 %slice_bitcast_fusion = (bf16[1,2048,384]{1,2,0:T(8,128)(2,1)S(1)}, bf16[1,2048,384]{1,2,0:T(8,128)(2,1)S(1)}) fusion(bf16[768,2048]{1,0:T(8,128)(2,1)} %get-tuple-element.11), kind=kLoop, calls=%fused_computation | loop fusion | bytes 6291456 | tf_op jit(solution)/shard_map/transpose | solution.py:585
  183.7 1.6 copy.16
  185.3 0.0 copy-start
  185.3 1.6 copy.15
  186.9 1.9 copy.19
  188.8 0.0 copy-done
  188.8 1.1 copy.20
Async XLA Ops:
  185.3 3.4 %copy-start = (bf16[384,2048]{1,0:T(8,128)(2,1)S(1)}, bf16[384,2048]{1,0:T(8,128)(2,1)}, u32[]{:S(2)}) copy-start(bf16[384,2048]{1,0:T(8,128)(2,1)} %get-tuple-element.12) | copy-start | bytes 4718596

commit v4 on v3

--- a/solution.py
+++ b/solution.py
@@ -132,7 +132,8 @@
     down_hbm,
     grad_tokens_ref,
     grad_routing_ref,
-    grad_pair_ref,
+    grad_gate_ref,
+    grad_up_ref,
     grad_down_ref,
     rows_all,
     partial,
@@ -258,16 +259,16 @@
             device_id_type=pl.DeviceIdType.MESH,
         )
 
-    def half_rows(o, half):
-        start = o * block + half * (block // 2)
-        return pl.ds(pl.multiple_of(start, block // 2), block // 2)
-
-    def chain_copy(zo, way, target, half):
+    def quarter_rows(o, quarter):
+        start = o * block + quarter * (block // 4)
+        return pl.ds(pl.multiple_of(start, block // 4), block // 4)
+
+    def chain_copy(zo, way, target, quarter):
         return pltpu.make_async_remote_copy(
-            src_ref=partial.at[half_rows(zo * 4 + y * 2 + c, half), :],
-            dst_ref=(rise_in if way == 0 else fall_in).at[half_rows(zo, half), :],
-            send_sem=chain_send.at[way, zo, half],
-            recv_sem=chain_recv.at[way, zo, half],
+            src_ref=partial.at[quarter_rows(zo * 4 + y * 2 + c, quarter), :],
+            dst_ref=(rise_in if way == 0 else fall_in).at[quarter_rows(zo, quarter), :],
+            send_sem=chain_send.at[way, zo, quarter],
+            recv_sem=chain_recv.at[way, zo, quarter],
             device_id={"ep": target},
             device_id_type=pl.DeviceIdType.MESH,
         )
@@ -346,18 +347,18 @@
         own = zo * 4 + y * 2 + c
 
         def pass_on(way, target, inner, source):
-            @pl.loop(0, 2)
-            def _(half):
+            @pl.loop(0, 4)
+            def _(quarter):
                 @pl.when(inner)
                 def _():
-                    chain_copy(zo, way, target, half).wait_recv()
-                    rows = half_rows(own, half)
+                    chain_copy(zo, way, target, quarter).wait_recv()
+                    rows = quarter_rows(own, quarter)
                     total = partial[rows, :].astype(jnp.float32) + source[
-                        half_rows(zo, half), :
+                        quarter_rows(zo, quarter), :
                     ].astype(jnp.float32)
                     partial[rows, :] = total.astype(jnp.bfloat16)
 
-                chain_copy(zo, way, target, half).start()
+                chain_copy(zo, way, target, quarter).start()
 
         @pl.when(zo > z)
         def _():
@@ -374,9 +375,11 @@
         def _(tile):
             start = pl.multiple_of(tile * tile_width, tile_width)
             span = pl.ds(start, tile_width)
-            grad_pair_ref[:, span] = jnp.dot(
+            pair = jnp.dot(
                 pair_t[...], rows_all[:, span], preferred_element_type=jnp.float32
             ).astype(jnp.bfloat16)
+            grad_gate_ref[:, span] = pair[:hidden_width]
+            grad_up_ref[:, span] = pair[hidden_width:]
             grad_down_ref[:, span] = jnp.dot(
                 hidden_t[...],
                 rows_all[:, pl.ds(pl.multiple_of(start + width, tile_width), tile_width)],
@@ -458,6 +461,8 @@
     def _():
         chain_copy(z, 0, above, 0).wait_recv()
         chain_copy(z, 0, above, 1).wait_recv()
+        chain_copy(z, 0, above, 2).wait_recv()
+        chain_copy(z, 0, above, 3).wait_recv()
 
     @pl.when(z == 0)
     def _():
@@ -467,6 +472,8 @@
     def _():
         chain_copy(z, 1, below, 0).wait_recv()
         chain_copy(z, 1, below, 1).wait_recv()
+        chain_copy(z, 1, below, 2).wait_recv()
+        chain_copy(z, 1, below, 3).wait_recv()
 
     @pl.when(z == depth - 1)
     def _():
@@ -517,11 +524,15 @@
         def _():
             chain_copy(zo, 0, above, 0).wait_send()
             chain_copy(zo, 0, above, 1).wait_send()
+            chain_copy(zo, 0, above, 2).wait_send()
+            chain_copy(zo, 0, above, 3).wait_send()
 
         @pl.when(zo < z)
         def _():
             chain_copy(zo, 1, below, 0).wait_send()
             chain_copy(zo, 1, below, 1).wait_send()
+            chain_copy(zo, 1, below, 2).wait_send()
+            chain_copy(zo, 1, below, 3).wait_send()
 
 
 def dense_local(tokens, cotangent, expert_ids, routing, gate_proj, up_proj, down_proj):
@@ -536,16 +547,17 @@
     vmem = pl.BlockSpec(memory_space=pltpu.VMEM)
     anywhere = pl.BlockSpec(memory_space=pl.ANY)
     dma = pltpu.SemaphoreType.DMA
-    grad_tokens, grad_routing, grad_pair, grad_down = pl.pallas_call(
+    grad_tokens, grad_routing, grad_gate, grad_up, grad_down = pl.pallas_call(
         functools.partial(expert_kernel, depth, first_rows),
         out_shape=(
             jax.ShapeDtypeStruct((block, width), bf16),
             jax.ShapeDtypeStruct((block, LANES), bf16),
-            jax.ShapeDtypeStruct((2 * hidden_width, width), bf16),
+            jax.ShapeDtypeStruct((hidden_width, width), bf16),
+            jax.ShapeDtypeStruct((hidden_width, width), bf16),
             jax.ShapeDtypeStruct((hidden_width, width), bf16),
         ),
         in_specs=[anywhere, anywhere, vmem, vmem, anywhere, anywhere, anywhere],
-        out_specs=(vmem, vmem, vmem, vmem),
+        out_specs=(vmem, vmem, vmem, vmem, vmem),
         scratch_shapes=[
             pltpu.VMEM((total, 2 * width + LANES), bf16),
             pltpu.VMEM((total, width + LANES), bf16),
@@ -565,8 +577,8 @@
             dma((2 * depth,)),
             dma((depth,)),
             dma((depth,)),
-            dma((2, depth, 2)),
-            dma((2, depth, 2)),
+            dma((2, depth, 4)),
+            dma((2, depth, 4)),
         ],
         compiler_params=pltpu.CompilerParams(
             collective_id=0, has_side_effects=True, vmem_limit_bytes=62 << 20
@@ -577,12 +589,11 @@
             transcendentals=total * hidden_width,
         ),
     )(tokens, cotangent, expert_ids, routing, gate_proj[0], up_proj[0], down_proj[0])
-    grad_pair = grad_pair.reshape(2, hidden_width, width)
     return (
         grad_tokens,
         grad_routing[:, :choose],
-        grad_pair[:1].transpose(0, 2, 1),
-        grad_pair[1:].transpose(0, 2, 1),
+        grad_gate.T[None],
+        grad_up.T[None],
         grad_down[None],
     )
 

time: 191 us -> 190 us (level)
    transpose x1 -> x0, local copies, waits for them, and re-layouts: 2.1 us -> none  [dense_local(): grad_pair[1:].transpose(0, 2, 1)]
    unnamed x9 -> x11, local copies, waits for them, and re-layouts: 10.4 us -> 11.5 us
where the time goes in v4:
time: 190 us; the launch traced here: 189 us
  Pallas kernels  177 us (93%)
  local copies, waits for them, and re-layouts  11.5 us (6%)
    pallas_call x1, Pallas kernels, dense_local(): pl.pallas_call(functools.partial(expert_kernel, depth, first_rows), out_s...  177 us
    unnamed x11, local copies, waits for them, and re-layouts  11.5 us

profile of v4, /device:TPU:0, one launch (start us, length us, event | category | flops | bytes accessed | tf_op | source)
XLA Modules:
  0.0 189.2 jit_solution(15687883500372175087)
XLA Ops:
  0.6 1.4 copy.13.routing_ref
  2.0 1.4 copy.12.ids_ref
  3.4 177.1 %shard_map.110 = (bf16[128,2048]{1,0:T(8,128)(2,1)}, bf16[128,128]{1,0:T(8,128)(2,1)}, bf16[384,2048]{1,0:T(8,128)(2,1)}, bf16[384,2048]{1,0:T(8,128)(2,1)}, bf16[384,2048]{1,0:T(8,128)(2,1)}) custom-call(bf16[128,2048]{1,0:T(8,128)(2,1)} %tokens_ref.1, bf16[128,2048]{1,0:T(8,128)(2,1)} %cotangent_ref.1, s32[128,8]{1,0:T(8,128)} %copy.12.ids_ref, ...), custom_call_target="tpu_custom_call" | custom-call | flops 25769803776 | bytes 15728640 | tf_op jit(solution)/shard_map/pallas_call | solution.py:550
  180.5 1.4 copy.14
  181.9 0.0 copy-start.1
  181.9 2.7 %copy.15 = bf16[1,2048,384]{2,1,0:T(8,128)(2,1)} copy(bf16[1,2048,384]{1,2,0:T(8,128)(2,1)} %bitcast.13) | data formatting | bytes 3145728
  184.6 0.0 copy-done.1
  184.6 0.0 copy-start
  184.6 1.6 copy.16
  186.2 1.9 copy.19
  188.1 0.0 copy-done
  188.1 1.1 copy.20
Async XLA Ops:
  181.9 2.7 %copy-start.1 = (bf16[384,2048]{1,0:T(8,128)(2,1)S(1)}, bf16[384,2048]{1,0:T(8,128)(2,1)}, u32[]{:S(2)}) copy-start(bf16[384,2048]{1,0:T(8,128)(2,1)} %get-tuple-element.13) | copy-start | bytes 4718596
  184.6 3.4 %copy-start = (bf16[384,2048]{1,0:T(8,128)(2,1)S(1)}, bf16[384,2048]{1,0:T(8,128)(2,1)}, u32[]{:S(2)}) copy-start(bf16[384,2048]{1,0:T(8,128)(2,1)} %get-tuple-element.14) | copy-start | bytes 4718596
